TPU v7x, 512 devices: a whole 4x8x8 slice. The times are simulated.
512 devices in a mesh: dp: 32 (over y, x), tensor: 16 (over z, core).
Axes of the slice: x: 4, y: 8, z: 8, core: 2. Of those that a mesh axis runs over, the one named last changes fastest.
Arguments:
- gradient: bfloat16 [32, 4096, 4096], P('dp', 'tensor'), may hold values from -20 to 20, as said below
- error_buffer: bfloat16 [32, 4096, 4096], P('dp', 'tensor'), may hold values from -1.5 to 1.5
- right_start: float32 [8, 4096], replicated, may hold values from -6 to 6
Outputs:
- update: float32 [4096, 4096], P('tensor', 'dp')
- left_factor: float32 [8, 4096], P(None, 'tensor')
- right_factor: float32 [8, 4096], replicated
Inputs may be any that keep to these rules, and one draw needn't show every extreme that they name: Entries of the gradient are real-valued with no zeros in bulk.
All inputs are finite; a program needn't handle non-finite values.
Results may differ from a plain program's by a relative error of at most 0.0003.
Values sent between devices are 32-bit elements; how exact they have to be, the bound alone decides.
No kernel may reach another device: no remote copies, remote signals or barrier semaphores. Data moves between devices by JAX's collectives and lax.ppermute only.
A program may use at most 64 MiB of HBM per device.

v0:
```python
import jax
import jax.numpy as jnp
from jax import lax
from jax.sharding import PartitionSpec as P


def lower_solve(chol, values):
    solved = []
    for index in range(chol.shape[0]):
        accum = values[index]
        for inner in range(index):
            accum = accum - chol[index, inner] * solved[inner]
        solved.append(accum / chol[index, index])
    return jnp.stack(solved)


def on_device(gradient, error_buffer, right_start):
    high = lax.Precision.HIGHEST
    corrected = gradient[0].astype(jnp.float32) + error_buffer[0].astype(jnp.float32)
    left_local = jnp.dot(right_start, corrected.T, precision=high)
    left_rows = lax.psum(left_local, "dp")
    gram = lax.psum(jnp.dot(left_rows, left_rows.T, precision=high), "tensor")
    chol = jnp.linalg.cholesky(gram)
    left_factor = lower_solve(chol, left_rows)
    right_local = jnp.dot(left_factor, corrected, precision=high)
    replicas = lax.axis_size("dp")
    right_factor = lax.psum(right_local, ("dp", "tensor")) / replicas
    column_count = right_factor.shape[1] // replicas
    column_start = lax.axis_index("dp") * column_count
    right_block = lax.dynamic_slice_in_dim(right_factor, column_start, column_count, 1)
    update = jnp.dot(left_factor.T, right_block, precision=high)
    return (update, left_factor, right_factor)


def solution(mesh):
    return jax.shard_map(
        on_device,
        mesh=mesh,
        in_specs=(P("dp", "tensor", None), P("dp", "tensor", None), P()),
        out_specs=(P("tensor", "dp"), P(None, "tensor"), P()),
        check_vma=False,
    )
```

profile of v0, /device:TPU:1, one launch (start us, length us, event | category | flops | bytes accessed | tf_op | source)
XLA Modules:
  0.0 415.9 jit_solution(838563310381710725)
XLA Ops:
  7.2 0.0 copy-start
  7.2 0.0 copy-start.1
  7.2 0.0 all-reduce.2.cloned.1.call-start
  7.2 0.8 copy-done
  8.1 5.7 %fusion.4 = f32[8,256]{1,0:T(8,128)S(1)} fusion(f32[8,4096]{1,0:T(8,128)S(1)} %copy-done, bf16[1,256,4096]{2,1,0:T(8,128)(2,1)} %param.4, bf16[1,256,4096]{2,1,0:T(8,128)(2,1)} %param.3), kind=kOutput, calls=%fused_computation.5 | convolution fusion | flops 103809024 | bytes 4333568 | tf_op jit(solution)/shard_map/dot_general | solution.py:20
  13.8 63.6 %psum.21 = f32[8,256]{1,0:T(8,128)S(1)} all-reduce(f32[8,256]{1,0:T(8,128)S(1)} %fusion.4), channel_id=1, replica_groups=mesh['dp'=32,'tensor'=16] {'dp'}, use_global_device_ids=true, to_apply=%region_0.0 | all-reduce | flops 2048 | bytes 16384 | tf_op jit(solution)/shard_map/psum | solution.py:21
  77.4 0.1 fusion.30
  77.5 43.3 %psum.22 = f32[8,8]{0,1:T(8,128)S(1)} all-reduce(f32[8,8]{0,1:T(8,128)S(1)} %fusion.30), channel_id=1, replica_groups=mesh['dp'=32,'tensor'=16] {'tensor'}, use_global_device_ids=true, to_apply=%region_1.0 | all-reduce | flops 64 | bytes 512 | tf_op jit(solution)/shard_map/psum | solution.py:22
  120.8 0.1 copy.7
  120.9 0.7 cholesky.18
  121.7 0.6 compare_reduce_fusion
  122.3 0.6 select_select_fusion
  123.0 0.7 fusion.28
  123.7 0.7 fusion.29
  124.4 22.7 %subtract_divide_fusion = (f32[1,256]{1,0:T(1,128)S(1)}, f32[1,256]{1,0:T(1,128)S(1)}, f32[1,256]{1,0:T(1,128)S(1)}, f32[1,256]{1,0:T(1,128)S(1)}, f32[1,256]{1,...) fusion(f32[8,256]{1,0:T(8,128)S(1)} %psum.21, f32[]{:T(128)} %bitcast.38, ...), kind=kLoop, calls=%fused_computation.36 | loop fusion | flops 16384 | bytes 16528 | tf_op jit(solution)/shard_map/div | solution.py:13
  147.1 0.0 copy-done.1
  147.1 0.0 copy-start.3
  147.1 4.7 %fusion = f32[8,4096]{1,0:T(8,128)} fusion(f32[8,256]{1,0:T(8,128)S(1)} %stack.2, bf16[1,256,4096]{2,1,0:T(8,128)(2,1)S(1)} %copy-done.1, bf16[1,256,4096]{2,1,0:T(8,128)(2,1)} %param.3), kind=kOutput, calls=%fused_computation | convolution fusion | flops 103809024 | bytes 4333568 | tf_op jit(solution)/shard_map/dot_general | solution.py:25
  151.8 0.0 all-reduce.2.cloned.1.call-update
  151.8 255.2 %all-reduce.2.cloned.1.call-done = f32[8,4096]{1,0:T(8,128)} async-done(((f32[8,4096]{1,0:T(8,128)}), f32[8,4096]{1,0:T(8,128)}) %all-reduce.2.cloned.1.call-update) | async-done | bytes 131088 | tf_op jit(solution)/shard_map/psum | solution.py:27
  407.0 0.9 broadcast_multiply_fusion
  407.9 0.0 copy-done.3
  407.9 0.0 copy-start.2
  408.0 1.1 fusion.8
  409.0 0.0 copy-done.2
  (3 shorter events, 0.1 us)
Async XLA Ops:
  7.2 0.9 copy-start
  7.2 139.9 %copy-start.1 = (bf16[1,256,4096]{2,1,0:T(8,128)(2,1)S(1)}, bf16[1,256,4096]{2,1,0:T(8,128)(2,1)}, u32[]{:S(2)}) copy-start(bf16[1,256,4096]{2,1,0:T(8,128)(2,1)} %param.4) | copy-start | bytes 6291460
  7.2 399.8 %all-reduce.2.cloned.1.call-start = ((), (), s32[]{:S(2)}) async-start(), calls=%async_computation | async-start | bytes 262144 | tf_op jit(solution)/shard_map/psum | solution.py:27
  147.1 260.8 %copy-start.3 = (f32[8,256]{1,0:T(8,128)}, f32[8,256]{1,0:T(8,128)S(1)}, u32[]{:S(2)}) copy-start(f32[8,256]{1,0:T(8,128)S(1)} %stack.2) | copy-start | bytes 24580
  407.9 1.1 copy-start.2
Sparse Core Ops, SparseCore 0:
  152.0 255.0 all-reduce.1
where the time goes:
time: 416 us
  waiting for transfers between devices  255 us (61%)
  blocking collectives  107 us (26%)
  other arithmetic  25.6 us (6%)
  between operations  14.1 us (3%)
  matrix products  11.5 us (3%)
    psum x1, waiting for transfers between devices, on_device(): right_factor = lax.psum(right_local, ('dp', 'tensor')) / replicas  255 us
    psum x1, blocking collectives, on_device(): left_rows = lax.psum(left_local, 'dp')  63.6 us
    psum x1, blocking collectives, on_device(): gram = lax.psum(jnp.dot(left_rows, left_rows.T, precision=high), 'tensor')  43.3 us
    div x1, other arithmetic, lower_solve(): solved.append(accum / chol[index, index])  22.7 us
  transfers between devices with their start and end apart: 1, of which 1 were waited for; matrix products, arithmetic and copies ran while one was open for 0% of the time, Pallas kernels for 0%

commit v1 on v0

v1 whole, which is shorter than its diff:
```python
import jax
import jax.numpy as jnp
from jax import lax
from jax.sharding import PartitionSpec as P

HIGH = lax.Precision.HIGHEST


def share(block, axis):
    count = lax.axis_size(axis)
    copies = jnp.broadcast_to(block[None], (count,) + block.shape)
    return lax.all_to_all(copies, axis, 0, 0)


def eliminate(gram, values):
    rank = gram.shape[0]
    rows = jnp.concatenate([gram, values], axis=1)
    index = jnp.arange(rank)[:, None]
    for step in range(rank):
        pivot_row = rows[step : step + 1] / jnp.sqrt(rows[step, step])
        factor = jnp.where(index > step, rows[:, step : step + 1] / jnp.sqrt(rows[step, step]), 0.0)
        rows = jnp.where(index == step, pivot_row, rows - factor * pivot_row)
    return rows[:, rank:]


def on_device(gradient, error_buffer, right_start):
    replicas, shards = lax.axis_size("dp"), lax.axis_size("tensor")
    rank, columns = right_start.shape
    corrected = gradient[0].astype(jnp.float32) + error_buffer[0].astype(jnp.float32)
    left_local = jnp.dot(right_start, corrected.T, precision=HIGH)
    left_sum = jnp.sum(share(left_local, "dp"), axis=0)
    gram_local = jnp.dot(left_sum, left_sum.T, precision=HIGH)
    raw_local = jnp.dot(left_sum, corrected, precision=HIGH)

    width = columns // shards
    blocks = jnp.swapaxes(raw_local.reshape(rank, shards, width), 0, 1)
    grams = jnp.broadcast_to(gram_local[None], (shards, rank, rank))
    grams = jnp.pad(grams, ((0, 0), (0, 0), (0, 128 - rank)))
    sent = jnp.concatenate([blocks, grams], axis=2)
    got = jnp.sum(lax.all_to_all(sent, "tensor", 0, 0), axis=0)
    raw_block, gram = got[:, :width], got[:, width : width + rank]
    raw_block = jnp.sum(share(raw_block, "dp"), axis=0)

    solved = eliminate(gram, jnp.concatenate([left_sum, raw_block / replicas], axis=1))
    left_factor, right_block = solved[:, : left_sum.shape[1]], solved[:, left_sum.shape[1] :]
    right_factor = jnp.swapaxes(share(right_block, "tensor"), 0, 1).reshape(rank, columns)
    column_count = columns // replicas
    right_own = lax.dynamic_slice_in_dim(right_factor, lax.axis_index("dp") * column_count, column_count, 1)
    update = jnp.dot(left_factor.T, right_own, precision=HIGH)
    return (update, left_factor, right_factor)


def solution(mesh):
    return jax.shard_map(
        on_device,
        mesh=mesh,
        in_specs=(P("dp", "tensor", None), P("dp", "tensor", None), P()),
        out_specs=(P("tensor", "dp"), P(None, "tensor"), P()),
        check_vma=False,
    )
```

time: 416 us -> 107 us (0.26)
  waiting for transfers between devices: 255 us -> 31.7 us
  blocking collectives: 107 us -> 0 us
  starting transfers between devices: 0.04 us -> 34.8 us
  other arithmetic: 25.6 us -> 7.28 us
  local copies, waits for them, and re-layouts: 2.41 us -> 14 us
  between operations: 14.1 us -> 6.4 us
    psum x1 -> x0, waiting for transfers between devices: 255 us -> none  [on_device(): right_factor = lax.psum(right_local, ('dp', 'tensor')) / replicas]
    psum x2 -> x0, blocking collectives: 107 us -> none  [the longest x1 63.6 us: on_device(): left_rows = lax.psum(left_local, 'dp')]
    all_to_all x0 -> x4, starting transfers between devices: none -> 34.8 us  [the longest x3 22.1 us: share(): return lax.all_to_all(copies, axis, 0, 0)]
    all_to_all x0 -> x4, waiting for transfers between devices: none -> 31.7 us  [the longest x3 21.4 us: share(): return lax.all_to_all(copies, axis, 0, 0)]
    div x3 -> x9, other arithmetic: 23.6 us -> 0.16 us  [the longest x8 0.15 us: eliminate(): pivot_row = rows[step:step + 1] / jnp.sqrt(rows[step, step])]
    dot_general x0 -> x1, local copies, waits for them, and re-layouts: none -> 5.6 us  [on_device(): raw_local = jnp.dot(left_sum, corrected, precision=HIGH)]
    dot_general x0 -> x1, other arithmetic: none -> 4.26 us  [on_device(): raw_local = jnp.dot(left_sum, corrected, precision=HIGH)]
  transfers between devices with their start and end apart: 1 -> 4, of which waited for: 1 -> 4; matrix products, arithmetic and copies ran while one was open for 0% -> 10% of each run, Pallas kernels for 0% -> 0%
where the time goes in v1:
time: 107 us
  starting transfers between devices  34.8 us (33%)
  waiting for transfers between devices  31.7 us (30%)
  local copies, waits for them, and re-layouts  14 us (13%)
  matrix products  12.5 us (12%)
  other arithmetic  7.28 us (7%)
  between operations  6.4 us (6%)
    all_to_all x3, starting transfers between devices, share(): return lax.all_to_all(copies, axis, 0, 0)  22.1 us
    all_to_all x3, waiting for transfers between devices, share(): return lax.all_to_all(copies, axis, 0, 0)  21.4 us
    all_to_all x1, starting transfers between devices, on_device(): got = jnp.sum(lax.all_to_all(sent, 'tensor', 0, 0), axis=0)  12.8 us
    all_to_all x1, waiting for transfers between devices, on_device(): got = jnp.sum(lax.all_to_all(sent, 'tensor', 0, 0), axis=0)  10.3 us
    dot_general x1, matrix products, on_device(): left_local = jnp.dot(right_start, corrected.T, precision=HIGH)  5.7 us
    dot_general x1, matrix products, on_device(): raw_local = jnp.dot(left_sum, corrected, precision=HIGH)  5.65 us
    dot_general x1, local copies, waits for them, and re-layouts, on_device(): raw_local = jnp.dot(left_sum, corrected, precision=HIGH)  5.6 us
    slice x8, local copies, waits for them, and re-layouts, eliminate(): pivot_row = rows[step:step + 1] / jnp.sqrt(rows[step, step])  4.61 us
  transfers between devices with their start and end apart: 4, of which 4 were waited for; matrix products, arithmetic and copies ran while one was open for 10% of the time, Pallas kernels for 0%

profile of v1, /device:TPU:1, one launch (start us, length us, event | category | flops | bytes accessed | tf_op | source)
XLA Modules:
  0.0 106.7 jit_solution(11972235315933029634)
XLA Ops:
  0.6 0.0 copy-start
  0.6 0.0 copy-start.1
  0.7 0.9 copy-done
  1.5 5.7 %fusion.3 = f32[8,256]{1,0:T(8,128)S(1)} fusion(f32[8,4096]{1,0:T(8,128)S(1)} %copy-done, bf16[1,256,4096]{2,1,0:T(8,128)(2,1)} %param.4, bf16[1,256,4096]{2,1,0:T(8,128)(2,1)} %param.3), kind=kOutput, calls=%fused_computation.5 | convolution fusion | flops 103809024 | bytes 4333568 | tf_op jit(solution)/shard_map/dot_general | solution.py:30
  7.2 0.7 broadcast_in_dim.146
  8.0 10.5 %all-to-all-start = ((f32[32,8,256]{2,1,0:T(8,128)}), f32[32,8,256]{2,1,0:T(8,128)S(1)}, u32[]{:S(2)}, u32[]{:S(2)}) async-start(f32[32,8,256]{2,1,0:T(8,128)} %broadcast_in_dim.146), calls=%async_computation | async-start | bytes 524288 | tf_op jit(solution)/shard_map/all_to_all | solution.py:12
  18.5 4.3 %fusion.2 = f32[4096,256]{0,1:T(8,128)} fusion(bf16[1,256,4096]{2,1,0:T(8,128)(2,1)S(1)} %copy-done.1, bf16[1,256,4096]{2,1,0:T(8,128)(2,1)} %param.3), kind=kLoop, calls=%fused_computation.3 | loop fusion | flops 3145728 | bytes 8388608 | tf_op jit(solution)/shard_map/dot_general | solution.py:33
  22.8 5.6 %copy.9 = f32[4096,256]{1,0:T(8,128)} copy(f32[4096,256]{0,1:T(8,128)} %fusion.2) | data formatting | bytes 8388608 | tf_op jit(solution)/shard_map/dot_general | solution.py:33
  28.4 1.3 %all-to-all-done = f32[32,8,256]{2,1,0:T(8,128)S(1)} async-done(((f32[32,8,256]{2,1,0:T(8,128)}), f32[32,8,256]{2,1,0:T(8,128)S(1)}, u32[]{:S(2)}, u32[]{:S(2)}) %all-to-all-start) | async-done | bytes 262176 | tf_op jit(solution)/shard_map/all_to_all | solution.py:12
  29.7 0.1 fusion.27
  29.9 5.6 %convolution_bitcast_fusion = f32[16,8,256]{2,1,0:T(8,128)S(1)} fusion(f32[16,256,256]{2,1,0:T(8,128)} %bitcast.32, f32[8,256]{1,0:T(8,128)S(1)} %reduce_sum.27), kind=kOutput, calls=%fused_computation.4 | convolution fusion | flops 100663296 | bytes 4333568 | tf_op jit(solution)/shard_map/dot_general | solution.py:33
  35.5 0.7 select_maximum_fusion
  36.2 12.8 %all-to-all-start.1 = ((f32[16,8,384]{2,1,0:T(8,128)}), f32[16,8,384]{2,1,0:T(8,128)S(1)}, u32[]{:S(2)}, u32[]{:S(2)}) async-start(f32[16,8,384]{2,1,0:T(8,128)} %select_maximum_fusion), calls=%async_computation.1 | async-start | bytes 393216 | tf_op jit(solution)/shard_map/all_to_all | solution.py:40
  49.0 10.3 %all-to-all-done.1 = f32[16,8,384]{2,1,0:T(8,128)S(1)} async-done(((f32[16,8,384]{2,1,0:T(8,128)}), f32[16,8,384]{2,1,0:T(8,128)S(1)}, u32[]{:S(2)}, u32[]{:S(2)}) %all-to-all-start.1) | async-done | bytes 196640 | tf_op jit(solution)/shard_map/all_to_all | solution.py:40
  59.4 0.7 broadcast_in_dim.148
  60.1 6.7 %all-to-all-start.2 = ((f32[32,8,256]{2,1,0:T(8,128)}), f32[32,8,256]{2,1,0:T(8,128)S(1)}, u32[]{:S(2)}, u32[]{:S(2)}) async-start(f32[32,8,256]{2,1,0:T(8,128)} %broadcast_in_dim.148), calls=%async_computation.2 | async-start | bytes 524288 | tf_op jit(solution)/shard_map/all_to_all | solution.py:12
  66.8 0.5 slice.128
  68.0 0.1 fusion.17
  68.1 10.9 %all-to-all-done.2 = f32[32,8,256]{2,1,0:T(8,128)S(1)} async-done(((f32[32,8,256]{2,1,0:T(8,128)}), f32[32,8,256]{2,1,0:T(8,128)S(1)}, u32[]{:S(2)}, u32[]{:S(2)}) %all-to-all-start.2) | async-done | bytes 262176 | tf_op jit(solution)/shard_map/all_to_all | solution.py:12
  79.1 0.1 pad_maximum_fusion
  79.2 0.1 subtract_select_fusion.7
  79.2 0.6 slice.131
  80.6 0.2 fusion.18
  80.7 0.1 subtract_select_fusion.6
  80.8 0.6 slice.134
  82.1 0.2 fusion.19
  82.3 0.1 subtract_select_fusion.5
  82.4 0.6 slice.137
  83.7 0.2 fusion.20
  83.9 0.1 subtract_select_fusion.4
  84.0 0.6 slice.140
  85.3 0.2 fusion.21
  85.4 0.1 subtract_select_fusion.3
  85.5 0.6 slice.143
  86.8 0.2 fusion.22
  87.0 0.1 subtract_select_fusion.2
  87.1 0.6 slice.146
  88.4 0.2 fusion.23
  88.6 0.1 subtract_select_fusion.1
  88.7 0.6 slice.149
  90.0 0.1 fusion.24
  90.1 0.1 subtract_select_fusion
  90.2 0.1 fusion.26
  90.3 0.7 broadcast_in_dim.166
  90.9 4.9 %all-to-all-start.3 = ((f32[16,8,256]{2,1,0:T(8,128)}), f32[16,8,256]{2,1,0:T(8,128)S(1)}, u32[]{:S(2)}, u32[]{:S(2)}) async-start(f32[16,8,256]{2,1,0:T(8,128)} %broadcast_in_dim.166), calls=%async_computation.3 | async-start | bytes 262144 | tf_op jit(solution)/shard_map/all_to_all | solution.py:12
  95.8 9.2 %all-to-all-done.3 = f32[16,8,256]{2,1,0:T(8,128)S(1)} async-done(((f32[16,8,256]{2,1,0:T(8,128)}), f32[16,8,256]{2,1,0:T(8,128)S(1)}, u32[]{:S(2)}, u32[]{:S(2)}) %all-to-all-start.3) | async-done | bytes 131104 | tf_op jit(solution)/shard_map/all_to_all | solution.py:12
  105.0 1.1 fusion.15
  106.1 0.7 copy.11
  (26 shorter events, 0.3 us)
Async XLA Ops:
  0.6 0.9 copy-start
  0.6 17.9 %copy-start.1 = (bf16[1,256,4096]{2,1,0:T(8,128)(2,1)S(1)}, bf16[1,256,4096]{2,1,0:T(8,128)(2,1)}, u32[]{:S(2)}) copy-start(bf16[1,256,4096]{2,1,0:T(8,128)(2,1)} %param.4) | copy-start | bytes 6291460
  8.0 21.7 %all-to-all-start = ((f32[32,8,256]{2,1,0:T(8,128)}), f32[32,8,256]{2,1,0:T(8,128)S(1)}, u32[]{:S(2)}, u32[]{:S(2)}) async-start(f32[32,8,256]{2,1,0:T(8,128)} %broadcast_in_dim.146), calls=%async_computation | async-start | bytes 524288 | tf_op jit(solution)/shard_map/all_to_all | solution.py:12
  36.2 23.1 %all-to-all-start.1 = ((f32[16,8,384]{2,1,0:T(8,128)}), f32[16,8,384]{2,1,0:T(8,128)S(1)}, u32[]{:S(2)}, u32[]{:S(2)}) async-start(f32[16,8,384]{2,1,0:T(8,128)} %select_maximum_fusion), calls=%async_computation.1 | async-start | bytes 393216 | tf_op jit(solution)/shard_map/all_to_all | solution.py:40
  60.1 19.0 %all-to-all-start.2 = ((f32[32,8,256]{2,1,0:T(8,128)}), f32[32,8,256]{2,1,0:T(8,128)S(1)}, u32[]{:S(2)}, u32[]{:S(2)}) async-start(f32[32,8,256]{2,1,0:T(8,128)} %broadcast_in_dim.148), calls=%async_computation.2 | async-start | bytes 524288 | tf_op jit(solution)/shard_map/all_to_all | solution.py:12
  90.3 16.5 %copy-start.2 = (f32[8,256]{1,0:T(8,128)}, f32[8,256]{1,0:T(8,128)S(1)}, u32[]{:S(2)}) copy-start(f32[8,256]{1,0:T(8,128)S(1)} %get-tuple-element.9) | copy-start | bytes 24580
  90.9 14.1 %all-to-all-start.3 = ((f32[16,8,256]{2,1,0:T(8,128)}), f32[16,8,256]{2,1,0:T(8,128)S(1)}, u32[]{:S(2)}, u32[]{:S(2)}) async-start(f32[16,8,256]{2,1,0:T(8,128)} %broadcast_in_dim.166), calls=%async_computation.3 | async-start | bytes 262144 | tf_op jit(solution)/shard_map/all_to_all | solution.py:12

commit v2 on v0

v2 whole, which is shorter than its diff:
```python
import functools

import jax
import jax.numpy as jnp
from jax import lax
from jax.experimental import pallas as pl
from jax.experimental.pallas import tpu as pltpu
from jax.sharding import PartitionSpec as P

HIGH = lax.Precision.HIGHEST
F32 = jnp.float32
BF16 = jnp.bfloat16
LANES = 128
VMEM = pl.BlockSpec(memory_space=pltpu.VMEM)
ANY = pl.BlockSpec(memory_space=pl.ANY)


def pieces(values):
    high = values.astype(BF16).astype(F32)
    rest = values - high
    middle = rest.astype(BF16).astype(F32)
    low = rest - middle
    none = jnp.zeros_like(values)
    return jnp.concatenate([high, middle, low, none], axis=0).astype(BF16)


def fold(products, rank):
    return products[:rank] + (products[rank : 2 * rank] + products[2 * rank : 3 * rank])


def left_kernel(chunks, gradient, error, start, out, gradient_here, error_here, arrived):
    copies = []
    rows = gradient.shape[0] // chunks
    for chunk in range(chunks):
        span = pl.ds(chunk * rows, rows)
        pair = []
        for which, (source, target) in enumerate(((gradient, gradient_here), (error, error_here))):
            copy = pltpu.make_async_copy(source.at[span], target.at[span], arrived.at[which, chunk])
            copy.start()
            pair.append(copy)
        copies.append(pair)
    rank = start.shape[0]
    cut = pieces(start[...])
    dims = (((1,), (1,)), ((), ()))
    for chunk in range(chunks):
        for copy in copies[chunk]:
            copy.wait()
        span = slice(chunk * rows, (chunk + 1) * rows)
        total = lax.dot_general(cut, gradient_here[span, :], dims, preferred_element_type=F32)
        total += lax.dot_general(cut, error_here[span, :], dims, preferred_element_type=F32)
        left = fold(total, rank)
        for copy in range(out.shape[0]):
            out[copy, :, span] = left


def left_terms(gradient, error, start, replicas):
    rows, columns = gradient.shape
    rank = start.shape[0]
    chunks = rows // LANES
    return pl.pallas_call(
        functools.partial(left_kernel, chunks),
        out_shape=jax.ShapeDtypeStruct((replicas, rank, rows), F32),
        in_specs=[ANY, ANY, VMEM],
        out_specs=VMEM,
        scratch_shapes=[
            pltpu.VMEM((rows, columns), BF16),
            pltpu.VMEM((rows, columns), BF16),
            pltpu.SemaphoreType.DMA((2, chunks)),
        ],
        compiler_params=pltpu.CompilerParams(vmem_limit_bytes=24 * 2**20),
        name="left_terms",
    )(gradient, error, start)


def raw_kernel(parts, gradient, error, sent, left_out):
    left = jnp.sum(parts[...], axis=0)
    left_out[...] = left
    rank, rows = left.shape
    shards = sent.shape[0]
    width = gradient.shape[1] // shards
    filled = jnp.concatenate([left, jnp.zeros((LANES - rank, rows), F32)], axis=0)
    gram = lax.dot_general(left, filled, (((1,), (1,)), ((), ())), precision=HIGH, preferred_element_type=F32)
    cut = pieces(left)
    for shard in range(shards):
        span = slice(shard * width, (shard + 1) * width)
        total = jnp.dot(cut, gradient[:, span], preferred_element_type=F32)
        total += jnp.dot(cut, error[:, span], preferred_element_type=F32)
        sent[shard, :, :width] = fold(total, rank)
        sent[shard, :, width:] = gram


def raw_terms(parts, gradient, error, shards):
    _, rank, rows = parts.shape
    width = gradient.shape[1] // shards
    return pl.pallas_call(
        raw_kernel,
        out_shape=(
            jax.ShapeDtypeStruct((shards, rank, width + LANES), F32),
            jax.ShapeDtypeStruct((rank, rows), F32),
        ),
        in_specs=[VMEM, VMEM, VMEM],
        out_specs=(VMEM, VMEM),
        compiler_params=pltpu.CompilerParams(vmem_limit_bytes=24 * 2**20),
        name="raw_terms",
    )(parts, gradient, error)


def block_kernel(parts, out, gram):
    total = jnp.sum(parts[...], axis=0)
    width = out.shape[2]
    for copy in range(out.shape[0]):
        out[copy] = total[:, :width]
    gram[...] = total[:, width:]


def block_sum(parts, replicas):
    _, rank, wide = parts.shape
    return pl.pallas_call(
        block_kernel,
        out_shape=(
            jax.ShapeDtypeStruct((replicas, rank, wide - LANES), F32),
            jax.ShapeDtypeStruct((rank, LANES), F32),
        ),
        in_specs=[VMEM],
        out_specs=(VMEM, VMEM),
        name="block_sum",
    )(parts)


def solve_kernel(parts, gram, left, out, left_out):
    replicas = parts.shape[0]
    block = jnp.sum(parts[...], axis=0) * (1.0 / replicas)
    rank, rows = left.shape
    table = jnp.concatenate([gram[...], left[...], block], axis=1)
    index = lax.broadcasted_iota(jnp.int32, table.shape, 0)
    for step in range(rank):
        scale = lax.rsqrt(table[step : step + 1, step : step + 1])
        pivot = table[step : step + 1, :] * scale
        factor = table[:, step : step + 1] * scale
        table = jnp.where(index > step, table - factor * pivot, jnp.where(index == step, pivot, table))
    left_out[...] = table[:, LANES : LANES + rows]
    for copy in range(out.shape[0]):
        out[copy] = table[:, LANES + rows :]


def solve(parts, gram, left, shards):
    _, rank, width = parts.shape
    return pl.pallas_call(
        solve_kernel,
        out_shape=(
            jax.ShapeDtypeStruct((shards, rank, width), F32),
            jax.ShapeDtypeStruct(left.shape, F32),
        ),
        in_specs=[VMEM, VMEM, VMEM],
        out_specs=(VMEM, VMEM),
        name="solve",
    )(parts, gram, left)


def update_kernel(parts, left, update, right):
    shards, _, width = parts.shape
    own = update.shape[1]
    each = width // own
    here = lax.axis_index("dp")
    offset = pl.multiple_of(lax.rem(here, each) * own, own)
    block = parts[here // each, :, pl.ds(offset, own)]
    update[...] = lax.dot_general(left[...], block, (((0,), (0,)), ((), ())), precision=HIGH, preferred_element_type=F32)
    for shard in range(shards):
        right[:, shard * width : (shard + 1) * width] = parts[shard]


def finish(parts, left, own):
    shards, rank, width = parts.shape
    return pl.pallas_call(
        update_kernel,
        out_shape=(
            jax.ShapeDtypeStruct((left.shape[1], own), F32),
            jax.ShapeDtypeStruct((rank, shards * width), F32),
        ),
        in_specs=[VMEM, VMEM],
        out_specs=(VMEM, VMEM),
        name="update",
    )(parts, left)


def on_device(gradient, error_buffer, right_start):
    replicas, shards = lax.axis_size("dp"), lax.axis_size("tensor")
    gradient, error = gradient[0], error_buffer[0]
    lefts = lax.all_to_all(left_terms(gradient, error, right_start, replicas), "dp", 0, 0)
    raws, left_sum = raw_terms(lefts, gradient, error, shards)
    blocks, gram = block_sum(lax.all_to_all(raws, "tensor", 0, 0), replicas)
    rights, left_factor = solve(lax.all_to_all(blocks, "dp", 0, 0), gram, left_sum, shards)
    update, right_factor = finish(lax.all_to_all(rights, "tensor", 0, 0), left_factor, right_start.shape[1] // replicas)
    return (update, left_factor, right_factor)


def solution(mesh):
    return jax.shard_map(
        on_device,
        mesh=mesh,
        in_specs=(P("dp", "tensor", None), P("dp", "tensor", None), P()),
        out_specs=(P("tensor", "dp"), P(None, "tensor"), P()),
        check_vma=False,
    )
```

time: 416 us -> 90.7 us (0.22)
  waiting for transfers between devices: 255 us -> 0 us
  blocking collectives: 107 us -> 75.5 us
  other arithmetic: 25.6 us -> 0 us
  between operations: 14.1 us -> 0.67 us
  matrix products: 11.5 us -> 0 us
  Pallas kernels: 0 us -> 9.44 us
    psum x1 -> x0, waiting for transfers between devices: 255 us -> none  [on_device(): right_factor = lax.psum(right_local, ('dp', 'tensor')) / replicas]
    psum x2 -> x0, blocking collectives: 107 us -> none  [the longest x1 63.6 us: on_device(): left_rows = lax.psum(left_local, 'dp')]
    all_to_all x0 -> x4, blocking collectives: none -> 75.5 us  [the longest x1 23 us: on_device(): blocks, gram = block_sum(lax.all_to_all(raws, 'tensor', 0, 0), replicas)]
    div x3 -> x0, other arithmetic: 23.6 us -> none  [the longest x1 22.7 us: lower_solve(): solved.append(accum / chol[index, index])]
    dot_general x4 -> x0, matrix products: 11.5 us -> none  [the longest x1 5.7 us: on_device(): left_local = jnp.dot(right_start, corrected.T, precision=high)]
    pallas_call x0 -> x5, Pallas kernels: none -> 9.44 us  [the longest x1 2.8 us: left_terms(): pl.pallas_call(functools.partial(left_kernel, chunks), out_shape=jax.Shap...]
  transfers between devices with their start and end apart: 1 -> 0, of which waited for: 1 -> 0; matrix products, arithmetic and copies ran while one was open for 0% -> 0% of each run, Pallas kernels for 0% -> 0%
where the time goes in v2:
time: 90.7 us; the launch traced here: 90.3 us
  blocking collectives  75.5 us (83%)
  Pallas kernels  9.44 us (10%)
  local copies, waits for them, and re-layouts  4.67 us (5%)
    all_to_all x1, blocking collectives, on_device(): blocks, gram = block_sum(lax.all_to_all(raws, 'tensor', 0, 0), replicas)  23 us
    all_to_all x1, blocking collectives, on_device(): lax.all_to_all(left_terms(gradient, error, right_start, replicas), 'dp',...  21.5 us
    all_to_all x1, blocking collectives, on_device(): lax.all_to_all(blocks, 'dp', 0, 0)  17.4 us
    all_to_all x1, blocking collectives, on_device(): lax.all_to_all(rights, 'tensor', 0, 0)  13.6 us
    unnamed x8, local copies, waits for them, and re-layouts  4.67 us
    pallas_call x1, Pallas kernels, left_terms(): pl.pallas_call(functools.partial(left_kernel, chunks), out_shape=jax.Shap...  2.8 us
    pallas_call x1, Pallas kernels, solve(): pl.pallas_call(solve_kernel, out_shape=(jax.ShapeDtypeStruct((shards, ran...  2.24 us
    pallas_call x1, Pallas kernels, finish(): pl.pallas_call(update_kernel, out_shape=(jax.ShapeDtypeStruct((left.shape...  1.89 us

profile of v2, /device:TPU:1, one launch (start us, length us, event | category | flops | bytes accessed | tf_op | source)
XLA Modules:
  0.0 90.3 jit_solution(2368415065624854575)
XLA Ops:
  0.6 0.0 copy-start
  0.6 1.6 %copy-done = bf16[1,256,4096]{2,1,0:T(8,128)(2,1)S(1)} copy-done((bf16[1,256,4096]{2,1,0:T(8,128)(2,1)S(1)}, bf16[1,256,4096]{2,1,0:T(8,128)(2,1)}, u32[]{:S(2)}) %copy-start) | copy-done | bytes 2097176
  2.2 0.0 copy-start.1
  2.2 1.6 %copy-done.1 = bf16[1,256,4096]{2,1,0:T(8,128)(2,1)S(1)} copy-done((bf16[1,256,4096]{2,1,0:T(8,128)(2,1)S(1)}, bf16[1,256,4096]{2,1,0:T(8,128)(2,1)}, u32[]{:S(2)}) %copy-start.1) | copy-done | bytes 2097176
  3.8 0.0 copy-start.2
  3.8 0.9 copy-done.2
  4.7 2.8 %left_terms.1 = f32[32,8,256]{2,1,0:T(8,128)S(1)} custom-call(bf16[256,4096]{1,0:T(8,128)(2,1)S(1)} %bitcast.2, bf16[256,4096]{1,0:T(8,128)(2,1)S(1)} %bitcast.4, f32[8,4096]{1,0:T(8,128)S(1)} %copy-done.2), custom_call_target="tpu_custom_call" | custom-call | tf_op jit(solution)/shard_map/left_terms/pallas_call | solution.py:60
  7.5 21.5 %all_to_all.20.parts = f32[32,8,256]{2,1,0:T(8,128)S(1)} all-to-all(f32[32,8,256]{2,1,0:T(8,128)S(1)} %left_terms.1), channel_id=1, replica_groups=mesh['dp'=32,'tensor'=16] {'dp'}, dimensions={0} | all-to-all | bytes 524288 | tf_op jit(solution)/shard_map/all_to_all | solution.py:189
  29.0 0.9 raw_terms.1
  29.9 0.0 copy-start.3
  29.9 0.6 copy-done.3
  30.5 23.0 %all_to_all.21.parts = f32[16,8,384]{2,1,0:T(8,128)} all-to-all(f32[16,8,384]{2,1,0:T(8,128)S(1)} %get-tuple-element.11), channel_id=1, replica_groups=mesh['dp'=32,'tensor'=16] {'tensor'}, dimensions={0} | all-to-all | bytes 393216 | tf_op jit(solution)/shard_map/all_to_all | solution.py:191
  53.5 1.7 %block_sum.1 = (f32[32,8,256]{2,1,0:T(8,128)}, f32[8,128]{1,0:T(8,128)}) custom-call(f32[16,8,384]{2,1,0:T(8,128)} %all_to_all.21.parts), custom_call_target="tpu_custom_call" | custom-call | tf_op jit(solution)/shard_map/block_sum/pallas_call | solution.py:118
  55.1 17.4 %all_to_all.22.parts = f32[32,8,256]{2,1,0:T(8,128)} all-to-all(f32[32,8,256]{2,1,0:T(8,128)} %get-tuple-element.12), channel_id=1, replica_groups=mesh['dp'=32,'tensor'=16] {'dp'}, dimensions={0} | all-to-all | bytes 524288 | tf_op jit(solution)/shard_map/all_to_all | solution.py:192
  72.5 2.2 %solve.1 = (f32[16,8,256]{2,1,0:T(8,128)}, f32[8,256]{1,0:T(8,128)}) custom-call(f32[32,8,256]{2,1,0:T(8,128)} %all_to_all.22.parts, f32[8,128]{1,0:T(8,128)} %get-tuple-element.13.gram, f32[8,256]{1,0:T(8,128)} %copy-done.3), custom_call_target="tpu_custom_call" | custom-call | tf_op jit(solution)/shard_map/solve/pallas_call | solution.py:148
  74.8 13.6 %all_to_all.23.parts = f32[16,8,256]{2,1,0:T(8,128)} all-to-all(f32[16,8,256]{2,1,0:T(8,128)} %get-tuple-element.15), channel_id=1, replica_groups=mesh['dp'=32,'tensor'=16] {'tensor'}, dimensions={0} | all-to-all | bytes 262144 | tf_op jit(solution)/shard_map/all_to_all | solution.py:193
  88.4 1.9 %update.1 = (f32[256,128]{1,0:T(8,128)}, f32[8,4096]{1,0:T(8,128)}) custom-call(f32[16,8,256]{2,1,0:T(8,128)} %all_to_all.23.parts, f32[8,256]{1,0:T(8,128)} %get-tuple-element.9.left), custom_call_target="tpu_custom_call" | custom-call | tf_op jit(solution)/shard_map/update/pallas_call | solution.py:174
Async XLA Ops:
  0.6 1.6 %copy-start = (bf16[1,256,4096]{2,1,0:T(8,128)(2,1)S(1)}, bf16[1,256,4096]{2,1,0:T(8,128)(2,1)}, u32[]{:S(2)}) copy-start(bf16[1,256,4096]{2,1,0:T(8,128)(2,1)} %param.3) | copy-start | bytes 6291460
  2.2 1.6 %copy-start.1 = (bf16[1,256,4096]{2,1,0:T(8,128)(2,1)S(1)}, bf16[1,256,4096]{2,1,0:T(8,128)(2,1)}, u32[]{:S(2)}) copy-start(bf16[1,256,4096]{2,1,0:T(8,128)(2,1)} %param.4) | copy-start | bytes 6291460
  3.8 0.9 %copy-start.2 = (f32[8,4096]{1,0:T(8,128)S(1)}, f32[8,4096]{1,0:T(8,128)}, u32[]{:S(2)}) copy-start(f32[8,4096]{1,0:T(8,128)} %start.1) | copy-start | bytes 393220
  29.9 0.6 copy-start.3

commit v3 on v2

v3 whole, which is shorter than its diff:
```python
import functools
import math

import jax
import jax.numpy as jnp
from jax import lax
from jax.experimental import pallas as pl
from jax.experimental.pallas import tpu as pltpu
from jax.sharding import Mesh
from jax.sharding import PartitionSpec as P

HIGH = lax.Precision.HIGHEST
F32 = jnp.float32
BF16 = jnp.bfloat16
LANES = 128
DP = ("yh", "yl", "x")
TENSOR = ("zh", "zl", "core")
NEAR = ("yl", "zl", "x", "core")
FAR = ("yh", "zh")
VMEM = pl.BlockSpec(memory_space=pltpu.VMEM)
SMALL = pltpu.CompilerParams(vmem_limit_bytes=16 * 2**20)


def pieces(values):
    high = values.astype(BF16).astype(F32)
    rest = values - high
    middle = rest.astype(BF16).astype(F32)
    low = rest - middle
    none = jnp.zeros_like(values)
    return jnp.concatenate([high, middle, low, none], axis=0).astype(BF16)


def fold(products, rank):
    return products[:rank] + (products[rank : 2 * rank] + products[2 * rank : 3 * rank])


def left_kernel(gradient, error, start, out, gradient_here, error_here, start_here, arrived):
    copies = []
    for index, (source, target) in enumerate(((start, start_here), (gradient, gradient_here), (error, error_here))):
        copies.append(pltpu.make_async_copy(source, target, arrived.at[index]))
        copies[-1].start()
    rank = start.shape[0]
    copies[0].wait()
    cut = pieces(start_here[...])
    dims = (((1,), (1,)), ((), ()))
    copies[1].wait()
    total = lax.dot_general(cut, gradient_here[...], dims, preferred_element_type=F32)
    copies[2].wait()
    total += lax.dot_general(cut, error_here[...], dims, preferred_element_type=F32)
    left = fold(total, rank)
    for copy in range(out.shape[0]):
        out[copy] = left


def left_terms(gradient, error, start, replicas):
    rows, columns = gradient.shape
    rank = start.shape[0]
    return pl.pallas_call(
        left_kernel,
        out_shape=(
            pltpu.VMEM((replicas, rank, rows), F32),
            pltpu.VMEM((rows, columns), BF16),
            pltpu.VMEM((rows, columns), BF16),
        ),
        in_specs=[pl.BlockSpec(memory_space=pltpu.HBM)] * 3,
        out_specs=(VMEM, VMEM, VMEM),
        scratch_shapes=[pltpu.VMEM((rank, columns), F32), pltpu.SemaphoreType.DMA((3,))],
        compiler_params=SMALL,
        name="left_terms",
    )(*(pltpu.with_memory_space_constraint(array, pltpu.HBM) for array in (gradient, error, start)))


def raw_kernel(parts, gradient, error, sent, left_out):
    left = jnp.sum(parts[...], axis=0)
    left_out[...] = left
    rank, rows = left.shape
    filled = jnp.concatenate([left, jnp.zeros((LANES - rank, rows), F32)], axis=0)
    gram = lax.dot_general(left, filled, (((1,), (1,)), ((), ())), precision=HIGH, preferred_element_type=F32)
    cut = pieces(left)
    width = gradient.shape[1] // sent.shape[0]
    step = 2 * width
    for pair in range(sent.shape[0] // 2):
        span = slice(pair * step, (pair + 1) * step)
        total = jnp.dot(cut, gradient[:, span], preferred_element_type=F32)
        total += jnp.dot(cut, error[:, span], preferred_element_type=F32)
        total = fold(total, rank)
        for half in range(2):
            sent[2 * pair + half, :, :width] = total[:, half * width : (half + 1) * width]
            sent[2 * pair + half, :, width:] = gram


def raw_terms(parts, gradient, error, blocks):
    _, rank, rows = parts.shape
    width = gradient.shape[1] // blocks
    return pl.pallas_call(
        raw_kernel,
        out_shape=(
            pltpu.VMEM((blocks, rank, width + LANES), F32),
            pltpu.VMEM((rank, rows), F32),
        ),
        in_specs=[VMEM, VMEM, VMEM],
        out_specs=(VMEM, VMEM),
        compiler_params=SMALL,
        name="raw_terms",
    )(parts, gradient, error)


def sum_kernel(parts, out):
    total = jnp.sum(parts[...], axis=0)
    for copy in range(out.shape[0]):
        out[copy] = total


def sum_copies(parts, copies):
    return pl.pallas_call(
        sum_kernel,
        out_shape=pltpu.VMEM((copies,) + parts.shape[1:], F32),
        in_specs=[VMEM],
        out_specs=VMEM,
        compiler_params=SMALL,
        name="sum_copies",
    )(parts)


def solve_kernel(replicas, parts, left, out, left_out):
    total = jnp.sum(parts[...], axis=0) * (1.0 / replicas)
    rank, rows = left.shape
    width = out.shape[2]
    table = jnp.concatenate([total[:, width:], left[...], total[:, :width]], axis=1)
    index = lax.broadcasted_iota(jnp.int32, table.shape, 0)
    for step in range(rank):
        scale = lax.rsqrt(table[step : step + 1, step : step + 1])
        pivot = table[step : step + 1, :] * scale
        factor = table[:, step : step + 1] * scale
        table = jnp.where(index > step, table - factor * pivot, jnp.where(index == step, pivot, table))
    left_out[...] = table[:, LANES : LANES + rows]
    for copy in range(out.shape[0]):
        out[copy] = table[:, LANES + rows :]


def solve(parts, left, blocks, replicas):
    _, rank, wide = parts.shape
    return pl.pallas_call(
        functools.partial(solve_kernel, replicas),
        out_shape=(
            pltpu.VMEM((blocks, rank, wide - LANES), F32),
            pltpu.VMEM(left.shape, F32),
        ),
        in_specs=[VMEM, VMEM],
        out_specs=(VMEM, VMEM),
        compiler_params=SMALL,
        name="solve",
    )(parts, left)


def update_kernel(parts, left, update, left_out, right):
    blocks, _, width = parts.shape
    here = 0
    for axis in DP:
        here = here * lax.axis_size(axis) + lax.axis_index(axis)
    update[...] = lax.dot_general(
        left[...], parts[here], (((0,), (0,)), ((), ())), precision=HIGH, preferred_element_type=F32
    )
    left_out[...] = left[...]
    for block in range(blocks):
        right[:, block * width : (block + 1) * width] = parts[block]


def finish(parts, left):
    blocks, rank, width = parts.shape
    return pl.pallas_call(
        update_kernel,
        out_shape=(
            jax.ShapeDtypeStruct((left.shape[1], width), F32),
            jax.ShapeDtypeStruct(left.shape, F32),
            jax.ShapeDtypeStruct((rank, blocks * width), F32),
        ),
        in_specs=[VMEM, VMEM],
        out_specs=(VMEM, VMEM, VMEM),
        compiler_params=SMALL,
        name="update",
    )(parts, left)


def exchange(blocks, axes):
    return lax.all_to_all(blocks, axes, 0, 0)


def on_device(gradient, error_buffer, right_start):
    replicas, blocks, far = (math.prod(lax.axis_size(axis) for axis in axes) for axes in (DP, NEAR, FAR))
    lefts, gradient, error = left_terms(gradient[0], error_buffer[0], right_start, replicas)
    raws, left_sum = raw_terms(exchange(lefts, DP), gradient, error, blocks)
    sums = sum_copies(exchange(raws, NEAR), far)
    rights, left_factor = solve(exchange(sums, FAR), left_sum, blocks, replicas)
    return finish(exchange(rights, NEAR), left_factor)


def solution(mesh):
    split = Mesh(mesh.devices.reshape(4, 2, 4, 4, 2, 2), ("yh", "yl", "x", "zh", "zl", "core"))
    return jax.shard_map(
        on_device,
        mesh=split,
        in_specs=(P(DP, TENSOR, None), P(DP, TENSOR, None), P()),
        out_specs=(P(TENSOR, DP), P(None, TENSOR), P()),
        check_vma=False,
    )
```

time: 90.7 us -> 77.7 us (0.86)
  blocking collectives: 75.5 us -> 70.6 us
  local copies, waits for them, and re-layouts: 4.67 us -> 0 us
  Pallas kernels: 9.44 us -> 6.2 us
    all_to_all x4, blocking collectives: 75.5 us -> 70.6 us  [exchange(): return lax.all_to_all(blocks, axes, 0, 0)]
    unnamed x8 -> x0, local copies, waits for them, and re-layouts: 4.67 us -> none
    pallas_call x4, Pallas kernels: 7.56 us -> 5.22 us  [the longest x1 3.67 us: left_terms(): pl.pallas_call(left_kernel, out_shape=(pltpu.VMEM((replicas, rank, rows),...]
where the time goes in v3:
time: 77.7 us; the launch traced here: 77.5 us
  blocking collectives  70.6 us (91%)
  Pallas kernels  6.2 us (8%)
    all_to_all x4, blocking collectives, exchange(): return lax.all_to_all(blocks, axes, 0, 0)  70.6 us
    pallas_call x1, Pallas kernels, left_terms(): pl.pallas_call(left_kernel, out_shape=(pltpu.VMEM((replicas, rank, rows),...  3.67 us

profile of v3, /device:TPU:1, one launch (start us, length us, event | category | flops | bytes accessed | tf_op | source)
XLA Modules:
  0.0 77.5 jit_solution(11743862675915018038)
XLA Ops:
  0.6 3.7 %left_terms.1 = (f32[32,8,256]{2,1,0:T(8,128)S(1)}, bf16[256,4096]{1,0:T(8,128)(2,1)S(1)}, bf16[256,4096]{1,0:T(8,128)(2,1)S(1)}) custom-call(bf16[256,4096]{1,0:T(8,128)(2,1)} %bitcast.2, bf16[256,4096]{1,0:T(8,128)(2,1)} %bitcast.3, f32[8,4096]{1,0:T(8,128)} %start.1), custom_call_target="tpu_custom_call" | custom-call | tf_op jit(solution)/shard_map/left_terms/pallas_call | solution.py:58
  4.3 21.5 %all_to_all.20.parts = f32[32,8,256]{2,1,0:T(8,128)S(1)} all-to-all(f32[32,8,256]{2,1,0:T(8,128)S(1)} %get-tuple-element.10), channel_id=1, replica_groups=mesh['yh'=4,'yl'=2,'x'=4,'zh'=4,'zl'=2,'core'=2] {'yh','yl','x'}, dimensions={0} | all-to-all | bytes 524288 | tf_op jit(solution)/shard_map/all_to_all | solution.py:186
  25.8 0.9 %raw_terms.1 = (f32[32,8,256]{2,1,0:T(8,128)S(1)}, f32[8,256]{1,0:T(8,128)S(1)}) custom-call(f32[32,8,256]{2,1,0:T(8,128)S(1)} %all_to_all.20.parts, bf16[256,4096]{1,0:T(8,128)(2,1)S(1)} %get-tuple-element.11.gradient, bf16[256,4096]{1,0:T(8,128)(2,1)S(1)} %get-tuple-element.12.error), custom_call_target="tpu_custom_call" | custom-call | tf_op jit(solution)/shard_map/raw_terms/pallas_call | solution.py:95
  26.7 15.7 %all_to_all.21.parts = f32[32,8,256]{2,1,0:T(8,128)S(1)} all-to-all(f32[32,8,256]{2,1,0:T(8,128)S(1)} %get-tuple-element.13), channel_id=1, replica_groups=mesh['yh'=4,'yl'=2,'x'=4,'zh'=4,'zl'=2,'core'=2] {'yl','zl','x','core'}, dimensions={0} | all-to-all | bytes 524288 | tf_op jit(solution)/shard_map/all_to_all | solution.py:186
  42.4 21.7 %all_to_all.22.parts = f32[16,8,256]{2,1,0:T(8,128)S(1)} all-to-all(f32[16,8,256]{2,1,0:T(8,128)S(1)} %sum_copies.1), channel_id=1, replica_groups=mesh['yh'=4,'yl'=2,'x'=4,'zh'=4,'zl'=2,'core'=2] {'yh','zh'}, dimensions={0} | all-to-all | bytes 262144 | tf_op jit(solution)/shard_map/all_to_all | solution.py:186
  64.1 0.6 solve.1
  64.8 11.7 %all_to_all.23.parts = f32[32,8,128]{2,1,0:T(8,128)S(1)} all-to-all(f32[32,8,128]{2,1,0:T(8,128)S(1)} %get-tuple-element.15), channel_id=1, replica_groups=mesh['yh'=4,'yl'=2,'x'=4,'zh'=4,'zl'=2,'core'=2] {'yl','zl','x','core'}, dimensions={0} | all-to-all | bytes 262144 | tf_op jit(solution)/shard_map/all_to_all | solution.py:186
  76.5 1.0 %update.1 = (f32[256,128]{1,0:T(8,128)}, f32[8,256]{1,0:T(8,128)}, f32[8,4096]{1,0:T(8,128)}) custom-call(f32[32,8,128]{2,1,0:T(8,128)S(1)} %all_to_all.23.parts, f32[8,256]{1,0:T(8,128)S(1)} %get-tuple-element.16.left), custom_call_target="tpu_custom_call" | custom-call | tf_op jit(solution)/shard_map/update/pallas_call | solution.py:171
  (1 shorter events, 0.0 us)

commit v4 on v3

--- a/solution.py
+++ b/solution.py
@@ -17,6 +17,7 @@
 TENSOR = ("zh", "zl", "core")
 NEAR = ("yl", "zl", "x", "core")
 FAR = ("yh", "zh")
+FIRST = {DP: 18, NEAR: 29, FAR: 11}
 VMEM = pl.BlockSpec(memory_space=pltpu.VMEM)
 SMALL = pltpu.CompilerParams(vmem_limit_bytes=16 * 2**20)
 
@@ -183,7 +184,9 @@
 
 
 def exchange(blocks, axes):
-    return lax.all_to_all(blocks, axes, 0, 0)
+    count = blocks.shape[0]
+    order = [(index + FIRST[axes]) % count for index in range(count)]
+    return lax.all_to_all(blocks, axes, 0, 0, axis_index_groups=[order])
 
 
 def on_device(gradient, error_buffer, right_start):

time: 77.7 us -> 68 us (0.88)
  blocking collectives: 70.6 us -> 60.9 us
    all_to_all x4, blocking collectives: 70.6 us -> 60.9 us  [exchange(): return lax.all_to_all(blocks, axes, 0, 0, axis_index_groups=[order])]
where the time goes in v4:
time: 68 us; the launch traced here: 67.7 us
  blocking collectives  60.9 us (90%)
  Pallas kernels  6.2 us (9%)
    all_to_all x4, blocking collectives, exchange(): return lax.all_to_all(blocks, axes, 0, 0, axis_index_groups=[order])  60.9 us
    pallas_call x1, Pallas kernels, left_terms(): pl.pallas_call(left_kernel, out_shape=(pltpu.VMEM((replicas, rank, rows),...  3.67 us

profile of v4, /device:TPU:1, one launch (start us, length us, event | category | flops | bytes accessed | tf_op | source)
XLA Modules:
  0.0 67.7 jit_solution(10431765960549939406)
XLA Ops:
  0.6 3.7 %left_terms.1 = (f32[32,8,256]{2,1,0:T(8,128)S(1)}, bf16[256,4096]{1,0:T(8,128)(2,1)S(1)}, bf16[256,4096]{1,0:T(8,128)(2,1)S(1)}) custom-call(bf16[256,4096]{1,0:T(8,128)(2,1)} %bitcast.2, bf16[256,4096]{1,0:T(8,128)(2,1)} %bitcast.3, f32[8,4096]{1,0:T(8,128)} %start.1), custom_call_target="tpu_custom_call" | custom-call | tf_op jit(solution)/shard_map/left_terms/pallas_call | solution.py:59
  4.3 15.8 %all_to_all.20.parts = f32[32,8,256]{2,1,0:T(8,128)S(1)} all-to-all(f32[32,8,256]{2,1,0:T(8,128)S(1)} %get-tuple-element.10), channel_id=1, replica_groups={{288,304,320,336,352,368,384,400,416,432,448,464,480,496,0,16,32,48,64,..., dimensions={0} | all-to-all | bytes 524288 | tf_op jit(solution)/shard_map/all_to_all | solution.py:189
  20.1 0.9 %raw_terms.1 = (f32[32,8,256]{2,1,0:T(8,128)S(1)}, f32[8,256]{1,0:T(8,128)S(1)}) custom-call(f32[32,8,256]{2,1,0:T(8,128)S(1)} %all_to_all.20.parts, bf16[256,4096]{1,0:T(8,128)(2,1)S(1)} %get-tuple-element.11.gradient, bf16[256,4096]{1,0:T(8,128)(2,1)S(1)} %get-tuple-element.12.error), custom_call_target="tpu_custom_call" | custom-call | tf_op jit(solution)/shard_map/raw_terms/pallas_call | solution.py:96
  21.0 15.8 %all_to_all.21.parts = f32[32,8,256]{2,1,0:T(8,128)S(1)} all-to-all(f32[32,8,256]{2,1,0:T(8,128)S(1)} %get-tuple-element.13), channel_id=1, replica_groups={{99,114,115,0,1,16,17,32,33,48,49,2,3,18,19,34,35,50,51,64,65,80,81,96,..., dimensions={0} | all-to-all | bytes 524288 | tf_op jit(solution)/shard_map/all_to_all | solution.py:189
  36.8 19.0 %all_to_all.22.parts = f32[16,8,256]{2,1,0:T(8,128)S(1)} all-to-all(f32[16,8,256]{2,1,0:T(8,128)S(1)} %sum_copies.1), channel_id=1, replica_groups={{268,384,388,392,396,0,4,8,12,128,132,136,140,256,260,264},{269,385,389..., dimensions={0} | all-to-all | bytes 262144 | tf_op jit(solution)/shard_map/all_to_all | solution.py:189
  55.9 0.6 solve.1
  56.5 10.2 %all_to_all.23.parts = f32[32,8,128]{2,1,0:T(8,128)S(1)} all-to-all(f32[32,8,128]{2,1,0:T(8,128)S(1)} %get-tuple-element.15), channel_id=1, replica_groups={{99,114,115,0,1,16,17,32,33,48,49,2,3,18,19,34,35,50,51,64,65,80,81,96,..., dimensions={0} | all-to-all | bytes 262144 | tf_op jit(solution)/shard_map/all_to_all | solution.py:189
  66.7 1.0 %update.1 = (f32[256,128]{1,0:T(8,128)}, f32[8,256]{1,0:T(8,128)}, f32[8,4096]{1,0:T(8,128)}) custom-call(f32[32,8,128]{2,1,0:T(8,128)S(1)} %all_to_all.23.parts, f32[8,256]{1,0:T(8,128)S(1)} %get-tuple-element.16.left), custom_call_target="tpu_custom_call" | custom-call | tf_op jit(solution)/shard_map/update/pallas_call | solution.py:172
  (1 shorter events, 0.0 us)

commit v5 on v3

--- a/solution.py
+++ b/solution.py
@@ -13,10 +13,18 @@
 F32 = jnp.float32
 BF16 = jnp.bfloat16
 LANES = 128
+GAP = 16
+
+
+def rotated(count, first):
+    return [(index + first) % count for index in range(count)]
+
+
 DP = ("yh", "yl", "x")
 TENSOR = ("zh", "zl", "core")
 NEAR = ("yl", "zl", "x", "core")
 FAR = ("yh", "zh")
+ORDERS = {"left": rotated(32, 22), "near": rotated(32, 29), "far": rotated(16, 11), "back": rotated(32, 29)}
 VMEM = pl.BlockSpec(memory_space=pltpu.VMEM)
 SMALL = pltpu.CompilerParams(vmem_limit_bytes=16 * 2**20)
 
@@ -74,28 +82,37 @@
     left = jnp.sum(parts[...], axis=0)
     left_out[...] = left
     rank, rows = left.shape
-    filled = jnp.concatenate([left, jnp.zeros((LANES - rank, rows), F32)], axis=0)
+    none = jnp.zeros((GAP - rank, rows), F32)
+    filled = jnp.concatenate([left, none] * (LANES // GAP), axis=0)
     gram = lax.dot_general(left, filled, (((1,), (1,)), ((), ())), precision=HIGH, preferred_element_type=F32)
+    gram_row = jnp.sum(jnp.where(own_lanes(gram.shape), gram, 0.0), axis=0, keepdims=True)
     cut = pieces(left)
-    width = gradient.shape[1] // sent.shape[0]
-    step = 2 * width
-    for pair in range(sent.shape[0] // 2):
+    step = 2 * LANES
+    high = rank + 1
+    for pair in range(gradient.shape[1] // step):
         span = slice(pair * step, (pair + 1) * step)
         total = jnp.dot(cut, gradient[:, span], preferred_element_type=F32)
         total += jnp.dot(cut, error[:, span], preferred_element_type=F32)
         total = fold(total, rank)
         for half in range(2):
-            sent[2 * pair + half, :, :width] = total[:, half * width : (half + 1) * width]
-            sent[2 * pair + half, :, width:] = gram
+            place = ORDERS["near"].index(ORDERS["back"][2 * pair + half])
+            start = place * high
+            sent[start : start + rank, :] = total[:, half * LANES : (half + 1) * LANES]
+            sent[start + rank : start + high, :] = gram_row
+
+
+def own_lanes(shape):
+    row = lax.broadcasted_iota(jnp.int32, shape, 0)
+    lane = lax.broadcasted_iota(jnp.int32, shape, 1)
+    return (lane >= row * GAP) & (lane < (row + 1) * GAP)
 
 
 def raw_terms(parts, gradient, error, blocks):
     _, rank, rows = parts.shape
-    width = gradient.shape[1] // blocks
     return pl.pallas_call(
         raw_kernel,
         out_shape=(
-            pltpu.VMEM((blocks, rank, width + LANES), F32),
+            pltpu.VMEM((blocks * (rank + 1), LANES), F32),
             pltpu.VMEM((rank, rows), F32),
         ),
         in_specs=[VMEM, VMEM, VMEM],
@@ -105,16 +122,26 @@
     )(parts, gradient, error)
 
 
-def sum_kernel(parts, out):
-    total = jnp.sum(parts[...], axis=0)
-    for copy in range(out.shape[0]):
-        out[copy] = total
-
-
-def sum_copies(parts, copies):
-    return pl.pallas_call(
-        sum_kernel,
-        out_shape=pltpu.VMEM((copies,) + parts.shape[1:], F32),
+def sum_blocks(parts, count):
+    high = parts.shape[0] // count
+    terms = [parts[index * high : (index + 1) * high, :] for index in range(count)]
+    while len(terms) > 1:
+        terms = [one + other for one, other in zip(terms[::2], terms[1::2])]
+    return terms[0]
+
+
+def sum_kernel(count, parts, out):
+    total = sum_blocks(parts, count)
+    high = total.shape[0]
+    for copy in range(out.shape[0] // high):
+        out[copy * high : (copy + 1) * high, :] = total
+
+
+def sum_copies(parts, count, copies):
+    high = parts.shape[0] // count
+    return pl.pallas_call(
+        functools.partial(sum_kernel, count),
+        out_shape=pltpu.VMEM((copies * high, LANES), F32),
         in_specs=[VMEM],
         out_specs=VMEM,
         compiler_params=SMALL,
@@ -122,11 +149,16 @@
     )(parts)
 
 
-def solve_kernel(replicas, parts, left, out, left_out):
-    total = jnp.sum(parts[...], axis=0) * (1.0 / replicas)
+def solve_kernel(replicas, count, parts, left, out, left_out):
+    total = sum_blocks(parts, count) * (1.0 / replicas)
     rank, rows = left.shape
-    width = out.shape[2]
-    table = jnp.concatenate([total[:, width:], left[...], total[:, :width]], axis=1)
+    gram = jnp.broadcast_to(total[rank:], (rank, LANES))
+    gram = jnp.where(own_lanes(gram.shape), gram, 0.0)
+    shift = LANES // 2
+    while shift >= GAP:
+        gram = gram + pltpu.roll(gram, shift, 1)
+        shift //= 2
+    table = jnp.concatenate([gram, left[...], total[:rank]], axis=1)
     index = lax.broadcasted_iota(jnp.int32, table.shape, 0)
     for step in range(rank):
         scale = lax.rsqrt(table[step : step + 1, step : step + 1])
@@ -138,12 +170,12 @@
         out[copy] = table[:, LANES + rows :]
 
 
-def solve(parts, left, blocks, replicas):
-    _, rank, wide = parts.shape
-    return pl.pallas_call(
-        functools.partial(solve_kernel, replicas),
-        out_shape=(
-            pltpu.VMEM((blocks, rank, wide - LANES), F32),
+def solve(parts, count, left, blocks, replicas):
+    rank = left.shape[0]
+    return pl.pallas_call(
+        functools.partial(solve_kernel, replicas, count),
+        out_shape=(
+            pltpu.VMEM((blocks, rank, LANES), F32),
             pltpu.VMEM(left.shape, F32),
         ),
         in_specs=[VMEM, VMEM],
@@ -182,17 +214,23 @@
     )(parts, left)
 
 
-def exchange(blocks, axes):
-    return lax.all_to_all(blocks, axes, 0, 0)
+def exchange(blocks, axes, order):
+    return lax.all_to_all(blocks, axes, 0, 0, axis_index_groups=[ORDERS[order]])
+
+
+def exchange_rows(rows, axes, order):
+    count = len(ORDERS[order])
+    high = rows.shape[0] // count
+    return exchange(rows.reshape(count, high, 1, LANES), axes, order).reshape(rows.shape)
 
 
 def on_device(gradient, error_buffer, right_start):
     replicas, blocks, far = (math.prod(lax.axis_size(axis) for axis in axes) for axes in (DP, NEAR, FAR))
     lefts, gradient, error = left_terms(gradient[0], error_buffer[0], right_start, replicas)
-    raws, left_sum = raw_terms(exchange(lefts, DP), gradient, error, blocks)
-    sums = sum_copies(exchange(raws, NEAR), far)
-    rights, left_factor = solve(exchange(sums, FAR), left_sum, blocks, replicas)
-    return finish(exchange(rights, NEAR), left_factor)
+    raws, left_sum = raw_terms(exchange(lefts, DP, "left"), gradient, error, blocks)
+    sums = sum_copies(exchange_rows(raws, NEAR, "near"), blocks, far)
+    rights, left_factor = solve(exchange_rows(sums, FAR, "far"), far, left_sum, blocks, replicas)
+    return finish(exchange(rights, NEAR, "back"), left_factor)
 
 
 def solution(mesh):

time: 77.7 us -> 65.6 us (0.84)
  blocking collectives: 70.6 us -> 58.2 us
    all_to_all x4, blocking collectives: 70.6 us -> 58.2 us  [exchange(): return lax.all_to_all(blocks, axes, 0, 0, axis_index_groups=[ORDERS[order]])]
where the time goes in v5:
time: 65.6 us; the launch traced here: 65.3 us
  blocking collectives  58.2 us (89%)
  Pallas kernels  6.39 us (10%)
  between operations  0.67 us (1%)
    all_to_all x4, blocking collectives, exchange(): return lax.all_to_all(blocks, axes, 0, 0, axis_index_groups=[ORDERS[order]])  58.2 us
    pallas_call x1, Pallas kernels, left_terms(): pl.pallas_call(left_kernel, out_shape=(pltpu.VMEM((replicas, rank, rows),...  3.67 us

profile of v5, /device:TPU:1, one launch (start us, length us, event | category | flops | bytes accessed | tf_op | source)
XLA Modules:
  0.0 65.3 jit_solution(11438910077996699742)
XLA Ops:
  0.6 3.7 %left_terms.1 = (f32[32,8,256]{2,1,0:T(8,128)S(1)}, bf16[256,4096]{1,0:T(8,128)(2,1)S(1)}, bf16[256,4096]{1,0:T(8,128)(2,1)S(1)}) custom-call(bf16[256,4096]{1,0:T(8,128)(2,1)} %bitcast.10, bf16[256,4096]{1,0:T(8,128)(2,1)} %bitcast.11, f32[8,4096]{1,0:T(8,128)} %start.1), custom_call_target="tpu_custom_call" | custom-call | tf_op jit(solution)/shard_map/left_terms/pallas_call | solution.py:66
  4.3 15.9 %all_to_all.20.parts = f32[32,8,256]{2,1,0:T(8,128)S(1)} all-to-all(f32[32,8,256]{2,1,0:T(8,128)S(1)} %get-tuple-element.10), channel_id=1, replica_groups={{352,368,384,400,416,432,448,464,480,496,0,16,32,48,64,80,96,112,128,14..., dimensions={0} | all-to-all | bytes 524288 | tf_op jit(solution)/shard_map/all_to_all | solution.py:218
  20.2 0.9 %raw_terms.1 = (f32[288,128]{1,0:T(8,128)S(1)}, f32[8,256]{1,0:T(8,128)S(1)}) custom-call(f32[32,8,256]{2,1,0:T(8,128)S(1)} %all_to_all.20.parts, bf16[256,4096]{1,0:T(8,128)(2,1)S(1)} %get-tuple-element.11.gradient, bf16[256,4096]{1,0:T(8,128)(2,1)S(1)} %get-tuple-element.12.error), custom_call_target="tpu_custom_call" | custom-call | tf_op jit(solution)/shard_map/raw_terms/pallas_call | solution.py:112
  21.1 14.4 %all_to_all.21 = f32[32,9,1,128]{3,2,1,0:T(1,128)S(1)} all-to-all(f32[32,9,1,128]{3,2,1,0:T(1,128)S(1)} %bitcast.9), channel_id=1, replica_groups={{99,114,115,0,1,16,17,32,33,48,49,2,3,18,19,34,35,50,51,64,65,80,81,96,..., dimensions={0} | all-to-all | bytes 294912 | tf_op jit(solution)/shard_map/all_to_all | solution.py:218
  35.5 17.5 %all_to_all.22 = f32[16,9,1,128]{3,2,1,0:T(1,128)S(1)} all-to-all(f32[16,9,1,128]{3,2,1,0:T(1,128)S(1)} %bitcast.7), channel_id=1, replica_groups={{268,384,388,392,396,0,4,8,12,128,132,136,140,256,260,264},{269,385,389..., dimensions={0} | all-to-all | bytes 147456 | tf_op jit(solution)/shard_map/all_to_all | solution.py:218
  53.0 0.8 %solve.1 = (f32[32,8,128]{2,1,0:T(8,128)S(1)}, f32[8,256]{1,0:T(8,128)S(1)}) custom-call(f32[144,128]{1,0:T(8,128)S(1)} %bitcast.8, f32[8,256]{1,0:T(8,128)S(1)} %get-tuple-element.14.left), custom_call_target="tpu_custom_call" | custom-call | tf_op jit(solution)/shard_map/solve/pallas_call | solution.py:175
  53.9 10.5 %all_to_all.23.parts = f32[32,8,128]{2,1,0:T(8,128)S(1)} all-to-all(f32[32,8,128]{2,1,0:T(8,128)S(1)} %get-tuple-element.15), channel_id=1, replica_groups={{99,114,115,0,1,16,17,32,33,48,49,2,3,18,19,34,35,50,51,64,65,80,81,96,..., dimensions={0} | all-to-all | bytes 262144 | tf_op jit(solution)/shard_map/all_to_all | solution.py:218
  64.3 1.0 %update.1 = (f32[256,128]{1,0:T(8,128)}, f32[8,256]{1,0:T(8,128)}, f32[8,4096]{1,0:T(8,128)}) custom-call(f32[32,8,128]{2,1,0:T(8,128)S(1)} %all_to_all.23.parts, f32[8,256]{1,0:T(8,128)S(1)} %get-tuple-element.16.left), custom_call_target="tpu_custom_call" | custom-call | tf_op jit(solution)/shard_map/update/pallas_call | solution.py:203
  (1 shorter events, 0.0 us)

commit v6 on v5

--- a/solution.py
+++ b/solution.py
@@ -43,19 +43,30 @@
 
 
 def left_kernel(gradient, error, start, out, gradient_here, error_here, start_here, arrived):
+    first = pltpu.make_async_copy(start, start_here, arrived.at[0])
+    first.start()
+    columns = gradient.shape[1]
+    edges = [0, columns // 4, columns * 5 // 8, columns]
+    spans = list(zip(edges[:-1], edges[1:]))
     copies = []
-    for index, (source, target) in enumerate(((start, start_here), (gradient, gradient_here), (error, error_here))):
-        copies.append(pltpu.make_async_copy(source, target, arrived.at[index]))
-        copies[-1].start()
-    rank = start.shape[0]
-    copies[0].wait()
-    cut = pieces(start_here[...])
-    dims = (((1,), (1,)), ((), ()))
-    copies[1].wait()
-    total = lax.dot_general(cut, gradient_here[...], dims, preferred_element_type=F32)
-    copies[2].wait()
-    total += lax.dot_general(cut, error_here[...], dims, preferred_element_type=F32)
-    left = fold(total, rank)
+    for index, (low, high) in enumerate(spans):
+        pair = []
+        for which, (source, target) in enumerate(((gradient, gradient_here), (error, error_here))):
+            span = pl.ds(low, high - low)
+            copy = pltpu.make_async_copy(source.at[:, span], target.at[:, span], arrived.at[1 + 2 * index + which])
+            copy.start()
+            pair.append(copy)
+        copies.append(pair)
+    first.wait()
+    cut = pieces(start_here[...]).astype(F32).T.astype(BF16)
+    total = 0.0
+    for (low, high), pair in zip(spans, copies):
+        for copy in pair:
+            copy.wait()
+        total += jnp.dot(gradient_here[:, low:high], cut[low:high], preferred_element_type=F32) + jnp.dot(
+            error_here[:, low:high], cut[low:high], preferred_element_type=F32
+        )
+    left = fold(total.T, start.shape[0])
     for copy in range(out.shape[0]):
         out[copy] = left
 
@@ -72,7 +83,7 @@
         ),
         in_specs=[pl.BlockSpec(memory_space=pltpu.HBM)] * 3,
         out_specs=(VMEM, VMEM, VMEM),
-        scratch_shapes=[pltpu.VMEM((rank, columns), F32), pltpu.SemaphoreType.DMA((3,))],
+        scratch_shapes=[pltpu.VMEM((rank, columns), F32), pltpu.SemaphoreType.DMA((7,))],
         compiler_params=SMALL,
         name="left_terms",
     )(*(pltpu.with_memory_space_constraint(array, pltpu.HBM) for array in (gradient, error, start)))
@@ -158,16 +169,23 @@
     while shift >= GAP:
         gram = gram + pltpu.roll(gram, shift, 1)
         shift //= 2
-    table = jnp.concatenate([gram, left[...], total[:rank]], axis=1)
-    index = lax.broadcasted_iota(jnp.int32, table.shape, 0)
+    spread = [jnp.broadcast_to(gram[:, column : column + 1], (rank, LANES)) for column in range(rank)]
+    values = [left[:, low : low + LANES] for low in range(0, rows, LANES)] + [total[:rank]]
+    index = lax.broadcasted_iota(jnp.int32, (rank, LANES), 0)
     for step in range(rank):
-        scale = lax.rsqrt(table[step : step + 1, step : step + 1])
-        pivot = table[step : step + 1, :] * scale
-        factor = table[:, step : step + 1] * scale
-        table = jnp.where(index > step, table - factor * pivot, jnp.where(index == step, pivot, table))
-    left_out[...] = table[:, LANES : LANES + rows]
+        scale = lax.rsqrt(spread[step][step : step + 1, :])
+        factor = spread[step] * scale
+
+        def eliminate(table):
+            pivot = table[step : step + 1, :] * scale
+            return jnp.where(index > step, table - factor * pivot, jnp.where(index == step, pivot, table))
+
+        spread = spread[: step + 1] + [eliminate(table) for table in spread[step + 1 :]]
+        values = [eliminate(table) for table in values]
+    for place, low in enumerate(range(0, rows, LANES)):
+        left_out[:, low : low + LANES] = values[place]
     for copy in range(out.shape[0]):
-        out[copy] = table[:, LANES + rows :]
+        out[copy] = values[-1]
 
 
 def solve(parts, count, left, blocks, replicas):

time: 65.6 us -> 64.4 us (0.982)
  Pallas kernels: 6.39 us -> 5.26 us
    pallas_call x1, Pallas kernels: 3.67 us -> 3.01 us  [left_terms(): pl.pallas_call(left_kernel, out_shape=(pltpu.VMEM((replicas, rank, rows),...]
where the time goes in v6:
time: 64.4 us; the launch traced here: 64.2 us
  blocking collectives  58.2 us (90%)
  Pallas kernels  5.26 us (8%)
  between operations  0.67 us (1%)
    all_to_all x4, blocking collectives, exchange(): return lax.all_to_all(blocks, axes, 0, 0, axis_index_groups=[ORDERS[order]])  58.2 us
    pallas_call x1, Pallas kernels, left_terms(): pl.pallas_call(left_kernel, out_shape=(pltpu.VMEM((replicas, rank, rows),...  3.01 us

profile of v6, /device:TPU:1, one launch (start us, length us, event | category | flops | bytes accessed | tf_op | source)
XLA Modules:
  0.0 64.2 jit_solution(3269468340213533127)
XLA Ops:
  0.6 3.0 %left_terms.1 = (f32[32,8,256]{2,1,0:T(8,128)S(1)}, bf16[256,4096]{1,0:T(8,128)(2,1)S(1)}, bf16[256,4096]{1,0:T(8,128)(2,1)S(1)}) custom-call(bf16[256,4096]{1,0:T(8,128)(2,1)} %bitcast.10, bf16[256,4096]{1,0:T(8,128)(2,1)} %bitcast.11, f32[8,4096]{1,0:T(8,128)} %start.1), custom_call_target="tpu_custom_call" | custom-call | tf_op jit(solution)/shard_map/left_terms/pallas_call | solution.py:77
  3.6 15.9 %all_to_all.20.parts = f32[32,8,256]{2,1,0:T(8,128)S(1)} all-to-all(f32[32,8,256]{2,1,0:T(8,128)S(1)} %get-tuple-element.10), channel_id=1, replica_groups={{352,368,384,400,416,432,448,464,480,496,0,16,32,48,64,80,96,112,128,14..., dimensions={0} | all-to-all | bytes 524288 | tf_op jit(solution)/shard_map/all_to_all | solution.py:236
  19.5 0.9 %raw_terms.1 = (f32[288,128]{1,0:T(8,128)S(1)}, f32[8,256]{1,0:T(8,128)S(1)}) custom-call(f32[32,8,256]{2,1,0:T(8,128)S(1)} %all_to_all.20.parts, bf16[256,4096]{1,0:T(8,128)(2,1)S(1)} %get-tuple-element.11.gradient, bf16[256,4096]{1,0:T(8,128)(2,1)S(1)} %get-tuple-element.12.error), custom_call_target="tpu_custom_call" | custom-call | tf_op jit(solution)/shard_map/raw_terms/pallas_call | solution.py:123
  20.4 14.4 %all_to_all.21 = f32[32,9,1,128]{3,2,1,0:T(1,128)S(1)} all-to-all(f32[32,9,1,128]{3,2,1,0:T(1,128)S(1)} %bitcast.9), channel_id=1, replica_groups={{99,114,115,0,1,16,17,32,33,48,49,2,3,18,19,34,35,50,51,64,65,80,81,96,..., dimensions={0} | all-to-all | bytes 294912 | tf_op jit(solution)/shard_map/all_to_all | solution.py:236
  34.8 17.5 %all_to_all.22 = f32[16,9,1,128]{3,2,1,0:T(1,128)S(1)} all-to-all(f32[16,9,1,128]{3,2,1,0:T(1,128)S(1)} %bitcast.7), channel_id=1, replica_groups={{268,384,388,392,396,0,4,8,12,128,132,136,140,256,260,264},{269,385,389..., dimensions={0} | all-to-all | bytes 147456 | tf_op jit(solution)/shard_map/all_to_all | solution.py:236
  52.4 0.4 solve.1
  52.7 10.5 %all_to_all.23.parts = f32[32,8,128]{2,1,0:T(8,128)S(1)} all-to-all(f32[32,8,128]{2,1,0:T(8,128)S(1)} %get-tuple-element.15), channel_id=1, replica_groups={{99,114,115,0,1,16,17,32,33,48,49,2,3,18,19,34,35,50,51,64,65,80,81,96,..., dimensions={0} | all-to-all | bytes 262144 | tf_op jit(solution)/shard_map/all_to_all | solution.py:236
  63.2 1.0 %update.1 = (f32[256,128]{1,0:T(8,128)}, f32[8,256]{1,0:T(8,128)}, f32[8,4096]{1,0:T(8,128)}) custom-call(f32[32,8,128]{2,1,0:T(8,128)S(1)} %all_to_all.23.parts, f32[8,256]{1,0:T(8,128)S(1)} %get-tuple-element.16.left), custom_call_target="tpu_custom_call" | custom-call | tf_op jit(solution)/shard_map/update/pallas_call | solution.py:221
  (1 shorter events, 0.0 us)

commit v7 on v6

--- a/solution.py
+++ b/solution.py
@@ -36,6 +36,18 @@
     low = rest - middle
     none = jnp.zeros_like(values)
     return jnp.concatenate([high, middle, low, none], axis=0).astype(BF16)
+
+
+def stacked(one, other, axis):
+    cuts = []
+    for values in (one, other):
+        high = values.astype(BF16).astype(F32)
+        middle = (values - high).astype(BF16).astype(F32)
+        cuts.append((high, middle, values - high - middle))
+    (high, middle, low), (high2, middle2, low2) = cuts
+    first = jnp.concatenate([high, high, middle, high, low, middle], axis=axis)
+    second = jnp.concatenate([high2, middle2, high2, low2, high2, middle2], axis=axis)
+    return first.astype(BF16), second.astype(BF16)
 
 
 def fold(products, rank):
@@ -208,9 +220,8 @@
     here = 0
     for axis in DP:
         here = here * lax.axis_size(axis) + lax.axis_index(axis)
-    update[...] = lax.dot_general(
-        left[...], parts[here], (((0,), (0,)), ((), ())), precision=HIGH, preferred_element_type=F32
-    )
+    first, second = stacked(left[...], parts[here], 0)
+    update[...] = lax.dot_general(first, second, (((0,), (0,)), ((), ())), preferred_element_type=F32)
     left_out[...] = left[...]
     for block in range(blocks):
         right[:, block * width : (block + 1) * width] = parts[block]

time: 64.4 us -> 64.3 us (level)
  no operation moved by 1% of the time
where the time goes in v7:
time: 64.3 us; the launch traced here: 64 us
  blocking collectives  58.2 us (91%)
  Pallas kernels  5.13 us (8%)
  between operations  0.67 us (1%)
    all_to_all x4, blocking collectives, exchange(): return lax.all_to_all(blocks, axes, 0, 0, axis_index_groups=[ORDERS[order]])  58.2 us
    pallas_call x1, Pallas kernels, left_terms(): pl.pallas_call(left_kernel, out_shape=(pltpu.VMEM((replicas, rank, rows),...  3.01 us

profile of v7, /device:TPU:1, one launch (start us, length us, event | category | flops | bytes accessed | tf_op | source)
XLA Modules:
  0.0 64.0 jit_solution(5179762220069834198)
XLA Ops:
  0.6 3.0 %left_terms.1 = (f32[32,8,256]{2,1,0:T(8,128)S(1)}, bf16[256,4096]{1,0:T(8,128)(2,1)S(1)}, bf16[256,4096]{1,0:T(8,128)(2,1)S(1)}) custom-call(bf16[256,4096]{1,0:T(8,128)(2,1)} %bitcast.10, bf16[256,4096]{1,0:T(8,128)(2,1)} %bitcast.11, f32[8,4096]{1,0:T(8,128)} %start.1), custom_call_target="tpu_custom_call" | custom-call | tf_op jit(solution)/shard_map/left_terms/pallas_call | solution.py:89
  3.6 15.9 %all_to_all.20.parts = f32[32,8,256]{2,1,0:T(8,128)S(1)} all-to-all(f32[32,8,256]{2,1,0:T(8,128)S(1)} %get-tuple-element.10), channel_id=1, replica_groups={{352,368,384,400,416,432,448,464,480,496,0,16,32,48,64,80,96,112,128,14..., dimensions={0} | all-to-all | bytes 524288 | tf_op jit(solution)/shard_map/all_to_all | solution.py:247
  19.5 0.9 %raw_terms.1 = (f32[288,128]{1,0:T(8,128)S(1)}, f32[8,256]{1,0:T(8,128)S(1)}) custom-call(f32[32,8,256]{2,1,0:T(8,128)S(1)} %all_to_all.20.parts, bf16[256,4096]{1,0:T(8,128)(2,1)S(1)} %get-tuple-element.11.gradient, bf16[256,4096]{1,0:T(8,128)(2,1)S(1)} %get-tuple-element.12.error), custom_call_target="tpu_custom_call" | custom-call | tf_op jit(solution)/shard_map/raw_terms/pallas_call | solution.py:135
  20.4 14.4 %all_to_all.21 = f32[32,9,1,128]{3,2,1,0:T(1,128)S(1)} all-to-all(f32[32,9,1,128]{3,2,1,0:T(1,128)S(1)} %bitcast.9), channel_id=1, replica_groups={{99,114,115,0,1,16,17,32,33,48,49,2,3,18,19,34,35,50,51,64,65,80,81,96,..., dimensions={0} | all-to-all | bytes 294912 | tf_op jit(solution)/shard_map/all_to_all | solution.py:247
  34.8 17.5 %all_to_all.22 = f32[16,9,1,128]{3,2,1,0:T(1,128)S(1)} all-to-all(f32[16,9,1,128]{3,2,1,0:T(1,128)S(1)} %bitcast.7), channel_id=1, replica_groups={{268,384,388,392,396,0,4,8,12,128,132,136,140,256,260,264},{269,385,389..., dimensions={0} | all-to-all | bytes 147456 | tf_op jit(solution)/shard_map/all_to_all | solution.py:247
  52.4 0.4 solve.1
  52.7 10.5 %all_to_all.23.parts = f32[32,8,128]{2,1,0:T(8,128)S(1)} all-to-all(f32[32,8,128]{2,1,0:T(8,128)S(1)} %get-tuple-element.15), channel_id=1, replica_groups={{99,114,115,0,1,16,17,32,33,48,49,2,3,18,19,34,35,50,51,64,65,80,81,96,..., dimensions={0} | all-to-all | bytes 262144 | tf_op jit(solution)/shard_map/all_to_all | solution.py:247
  63.2 0.9 %update.1 = (f32[256,128]{1,0:T(8,128)}, f32[8,256]{1,0:T(8,128)}, f32[8,4096]{1,0:T(8,128)}) custom-call(f32[32,8,128]{2,1,0:T(8,128)S(1)} %all_to_all.23.parts, f32[8,256]{1,0:T(8,128)S(1)} %get-tuple-element.16.left), custom_call_target="tpu_custom_call" | custom-call | tf_op jit(solution)/shard_map/update/pallas_call | solution.py:232
  (1 shorter events, 0.0 us)

commit v8 on v7

--- a/solution.py
+++ b/solution.py
@@ -1,4 +1,5 @@
 import functools
+import itertools
 import math
 
 import jax
@@ -24,7 +25,16 @@
 TENSOR = ("zh", "zl", "core")
 NEAR = ("yl", "zl", "x", "core")
 FAR = ("yh", "zh")
-ORDERS = {"left": rotated(32, 22), "near": rotated(32, 29), "far": rotated(16, 11), "back": rotated(32, 29)}
+ALL = ("yh", "yl", "x", "zh", "zl", "core")
+def far_groups(even, odd):
+    groups = []
+    for yl, x, zl, core in itertools.product(range(2), range(4), range(2), range(2)):
+        order = rotated(16, odd if zl else even)
+        groups.append([((((place // 4 * 2 + yl) * 4 + x) * 4 + place % 4) * 2 + zl) * 2 + core for place in order])
+    return groups
+
+
+ORDERS = {"left": rotated(32, 22), "near": rotated(32, 29), "far": far_groups(11, 10), "back": rotated(32, 29)}
 VMEM = pl.BlockSpec(memory_space=pltpu.VMEM)
 SMALL = pltpu.CompilerParams(vmem_limit_bytes=16 * 2**20)
 
@@ -244,11 +254,13 @@
 
 
 def exchange(blocks, axes, order):
+    if order == "far":
+        return lax.all_to_all(blocks, ALL, 0, 0, axis_index_groups=ORDERS[order])
     return lax.all_to_all(blocks, axes, 0, 0, axis_index_groups=[ORDERS[order]])
 
 
 def exchange_rows(rows, axes, order):
-    count = len(ORDERS[order])
+    count = math.prod(lax.axis_size(axis) for axis in axes)
     high = rows.shape[0] // count
     return exchange(rows.reshape(count, high, 1, LANES), axes, order).reshape(rows.shape)
 

time: 64.3 us -> 64.2 us (level)
    all_to_all x4 -> x3, blocking collectives: 58.2 us -> 40.7 us  [exchange(): return lax.all_to_all(blocks, axes, 0, 0, axis_index_groups=[ORDERS[order]])]
    all_to_all x0 -> x1, blocking collectives: none -> 17.5 us  [exchange(): return lax.all_to_all(blocks, ALL, 0, 0, axis_index_groups=ORDERS[order])]
where the time goes in v8:
time: 64.2 us; the launch traced here: 64 us
  blocking collectives  58.2 us (91%)
  Pallas kernels  5.13 us (8%)
  between operations  0.67 us (1%)
    all_to_all x3, blocking collectives, exchange(): return lax.all_to_all(blocks, axes, 0, 0, axis_index_groups=[ORDERS[order]])  40.7 us
    all_to_all x1, blocking collectives, exchange(): return lax.all_to_all(blocks, ALL, 0, 0, axis_index_groups=ORDERS[order])  17.5 us
    pallas_call x1, Pallas kernels, left_terms(): pl.pallas_call(left_kernel, out_shape=(pltpu.VMEM((replicas, rank, rows),...  3.01 us

profile of v8, /device:TPU:1, one launch (start us, length us, event | category | flops | bytes accessed | tf_op | source)
XLA Modules:
  0.0 64.0 jit_solution(5419205986736570814)
XLA Ops:
  0.6 3.0 %left_terms.1 = (f32[32,8,256]{2,1,0:T(8,128)S(1)}, bf16[256,4096]{1,0:T(8,128)(2,1)S(1)}, bf16[256,4096]{1,0:T(8,128)(2,1)S(1)}) custom-call(bf16[256,4096]{1,0:T(8,128)(2,1)} %bitcast.10, bf16[256,4096]{1,0:T(8,128)(2,1)} %bitcast.11, f32[8,4096]{1,0:T(8,128)} %start.1), custom_call_target="tpu_custom_call" | custom-call | tf_op jit(solution)/shard_map/left_terms/pallas_call | solution.py:99
  3.6 15.9 %all_to_all.20.parts = f32[32,8,256]{2,1,0:T(8,128)S(1)} all-to-all(f32[32,8,256]{2,1,0:T(8,128)S(1)} %get-tuple-element.10), channel_id=1, replica_groups={{352,368,384,400,416,432,448,464,480,496,0,16,32,48,64,80,96,112,128,14..., dimensions={0} | all-to-all | bytes 524288 | tf_op jit(solution)/shard_map/all_to_all | solution.py:259
  19.5 0.9 %raw_terms.1 = (f32[288,128]{1,0:T(8,128)S(1)}, f32[8,256]{1,0:T(8,128)S(1)}) custom-call(f32[32,8,256]{2,1,0:T(8,128)S(1)} %all_to_all.20.parts, bf16[256,4096]{1,0:T(8,128)(2,1)S(1)} %get-tuple-element.11.gradient, bf16[256,4096]{1,0:T(8,128)(2,1)S(1)} %get-tuple-element.12.error), custom_call_target="tpu_custom_call" | custom-call | tf_op jit(solution)/shard_map/raw_terms/pallas_call | solution.py:145
  20.4 14.4 %all_to_all.21 = f32[32,9,1,128]{3,2,1,0:T(1,128)S(1)} all-to-all(f32[32,9,1,128]{3,2,1,0:T(1,128)S(1)} %bitcast.9), channel_id=1, replica_groups={{99,114,115,0,1,16,17,32,33,48,49,2,3,18,19,34,35,50,51,64,65,80,81,96,..., dimensions={0} | all-to-all | bytes 294912 | tf_op jit(solution)/shard_map/all_to_all | solution.py:259
  34.8 17.5 %all_to_all.22 = f32[16,9,1,128]{3,2,1,0:T(1,128)S(1)} all-to-all(f32[16,9,1,128]{3,2,1,0:T(1,128)S(1)} %bitcast.7), channel_id=1, replica_groups={{268,384,388,392,396,0,4,8,12,128,132,136,140,256,260,264},{269,385,389..., dimensions={0} | all-to-all | bytes 147456 | tf_op jit(solution)/shard_map/all_to_all | solution.py:258
  52.4 0.4 solve.1
  52.7 10.4 %all_to_all.23.parts = f32[32,8,128]{2,1,0:T(8,128)S(1)} all-to-all(f32[32,8,128]{2,1,0:T(8,128)S(1)} %get-tuple-element.15), channel_id=1, replica_groups={{99,114,115,0,1,16,17,32,33,48,49,2,3,18,19,34,35,50,51,64,65,80,81,96,..., dimensions={0} | all-to-all | bytes 262144 | tf_op jit(solution)/shard_map/all_to_all | solution.py:259
  63.1 0.9 %update.1 = (f32[256,128]{1,0:T(8,128)}, f32[8,256]{1,0:T(8,128)}, f32[8,4096]{1,0:T(8,128)}) custom-call(f32[32,8,128]{2,1,0:T(8,128)S(1)} %all_to_all.23.parts, f32[8,256]{1,0:T(8,128)S(1)} %get-tuple-element.16.left), custom_call_target="tpu_custom_call" | custom-call | tf_op jit(solution)/shard_map/update/pallas_call | solution.py:242
  (1 shorter events, 0.0 us)

commit v9 on v8

--- a/solution.py
+++ b/solution.py
@@ -34,7 +34,7 @@
     return groups
 
 
-ORDERS = {"left": rotated(32, 22), "near": rotated(32, 29), "far": far_groups(11, 10), "back": rotated(32, 29)}
+ORDERS = {"left": rotated(32, 18), "near": rotated(32, 29), "far": far_groups(11, 10), "back": rotated(32, 29)}
 VMEM = pl.BlockSpec(memory_space=pltpu.VMEM)
 SMALL = pltpu.CompilerParams(vmem_limit_bytes=16 * 2**20)
 

time: 64.2 us -> 64.6 us (level)
  no operation moved by 1% of the time
where the time goes in v9:
time: 64.6 us; the launch traced here: 64.4 us
  blocking collectives  58.6 us (91%)
  Pallas kernels  5.13 us (8%)
  between operations  0.67 us (1%)
    all_to_all x3, blocking collectives, exchange(): return lax.all_to_all(blocks, axes, 0, 0, axis_index_groups=[ORDERS[order]])  40.8 us
    all_to_all x1, blocking collectives, exchange(): return lax.all_to_all(blocks, ALL, 0, 0, axis_index_groups=ORDERS[order])  17.8 us
    pallas_call x1, Pallas kernels, left_terms(): pl.pallas_call(left_kernel, out_shape=(pltpu.VMEM((replicas, rank, rows),...  3.01 us

profile of v9, /device:TPU:1, one launch (start us, length us, event | category | flops | bytes accessed | tf_op | source)
XLA Modules:
  0.0 64.4 jit_solution(17677083186189393369)
XLA Ops:
  0.6 3.0 %left_terms.1 = (f32[32,8,256]{2,1,0:T(8,128)S(1)}, bf16[256,4096]{1,0:T(8,128)(2,1)S(1)}, bf16[256,4096]{1,0:T(8,128)(2,1)S(1)}) custom-call(bf16[256,4096]{1,0:T(8,128)(2,1)} %bitcast.10, bf16[256,4096]{1,0:T(8,128)(2,1)} %bitcast.11, f32[8,4096]{1,0:T(8,128)} %start.1), custom_call_target="tpu_custom_call" | custom-call | tf_op jit(solution)/shard_map/left_terms/pallas_call | solution.py:99
  3.6 15.8 %all_to_all.20.parts = f32[32,8,256]{2,1,0:T(8,128)S(1)} all-to-all(f32[32,8,256]{2,1,0:T(8,128)S(1)} %get-tuple-element.10), channel_id=1, replica_groups={{288,304,320,336,352,368,384,400,416,432,448,464,480,496,0,16,32,48,64,..., dimensions={0} | all-to-all | bytes 524288 | tf_op jit(solution)/shard_map/all_to_all | solution.py:259
  19.5 0.9 %raw_terms.1 = (f32[288,128]{1,0:T(8,128)S(1)}, f32[8,256]{1,0:T(8,128)S(1)}) custom-call(f32[32,8,256]{2,1,0:T(8,128)S(1)} %all_to_all.20.parts, bf16[256,4096]{1,0:T(8,128)(2,1)S(1)} %get-tuple-element.11.gradient, bf16[256,4096]{1,0:T(8,128)(2,1)S(1)} %get-tuple-element.12.error), custom_call_target="tpu_custom_call" | custom-call | tf_op jit(solution)/shard_map/raw_terms/pallas_call | solution.py:145
  20.4 14.6 %all_to_all.21 = f32[32,9,1,128]{3,2,1,0:T(1,128)S(1)} all-to-all(f32[32,9,1,128]{3,2,1,0:T(1,128)S(1)} %bitcast.9), channel_id=1, replica_groups={{99,114,115,0,1,16,17,32,33,48,49,2,3,18,19,34,35,50,51,64,65,80,81,96,..., dimensions={0} | all-to-all | bytes 294912 | tf_op jit(solution)/shard_map/all_to_all | solution.py:259
  35.0 17.8 %all_to_all.22 = f32[16,9,1,128]{3,2,1,0:T(1,128)S(1)} all-to-all(f32[16,9,1,128]{3,2,1,0:T(1,128)S(1)} %bitcast.7), channel_id=1, replica_groups={{268,384,388,392,396,0,4,8,12,128,132,136,140,256,260,264},{269,385,389..., dimensions={0} | all-to-all | bytes 147456 | tf_op jit(solution)/shard_map/all_to_all | solution.py:258
  52.8 0.4 solve.1
  53.1 10.4 %all_to_all.23.parts = f32[32,8,128]{2,1,0:T(8,128)S(1)} all-to-all(f32[32,8,128]{2,1,0:T(8,128)S(1)} %get-tuple-element.15), channel_id=1, replica_groups={{99,114,115,0,1,16,17,32,33,48,49,2,3,18,19,34,35,50,51,64,65,80,81,96,..., dimensions={0} | all-to-all | bytes 262144 | tf_op jit(solution)/shard_map/all_to_all | solution.py:259
  63.5 0.9 %update.1 = (f32[256,128]{1,0:T(8,128)}, f32[8,256]{1,0:T(8,128)}, f32[8,4096]{1,0:T(8,128)}) custom-call(f32[32,8,128]{2,1,0:T(8,128)S(1)} %all_to_all.23.parts, f32[8,256]{1,0:T(8,128)S(1)} %get-tuple-element.16.left), custom_call_target="tpu_custom_call" | custom-call | tf_op jit(solution)/shard_map/update/pallas_call | solution.py:242
  (1 shorter events, 0.0 us)
